TPU v7x, 32 devices: a whole 2x2x4 slice. The times are simulated.
32 devices in a mesh: groups: 2 (over y), dom: 4 (over z), mp: 4 (over x, core).
Axes of the slice: x: 2, y: 2, z: 4, core: 2. Of those that a mesh axis runs over, the one named last changes fastest.
Arguments:
- node_latents: bfloat16 [1024, 512], P(('groups', 'dom')), parts along dimension 0, may hold values from -6 to 6
- edge_latents: bfloat16 [8192, 512], P(('groups', 'dom')), parts along dimension 0, may hold values from -6 to 6
- node_cotangent: bfloat16 [1024, 512], P(('groups', 'dom'), 'mp'), parts along dimension 0, may hold values from -6 to 6
- edge_cotangent: bfloat16 [8192, 512], P(('groups', 'dom'), 'mp'), parts along dimension 0, may hold values from -6 to 6
- senders: int32 [4096], P('dom'), may hold values from 0 to 255, as said below
- receivers: int32 [4096], P('dom'), may hold values from 0 to 127, as said below
- send_nodes: int32 [4, 4, 32], P('dom'), may hold values from 0 to 127, as said below
- edge_in_weight: bfloat16 [1536, 512], P(None, 'mp'), may hold values from -0.15625 to 0.15625
- edge_out_weight: bfloat16 [512, 512], P(None, 'mp'), may hold values from -0.25 to 0.25
- edge_gain: float32 [512], P('mp'), may hold values from 0.5 to 1.5
- node_in_weight: bfloat16 [1024, 512], P(None, 'mp'), may hold values from -0.1875 to 0.1875
- node_out_weight: bfloat16 [512, 512], P(None, 'mp'), may hold values from -0.25 to 0.25
- node_gain: float32 [512], P('mp'), may hold values from 0.5 to 1.5
Outputs:
- node_grad: bfloat16 [1024, 512], P(('groups', 'dom'), 'mp'), parts along dimension 0
- edge_grad: bfloat16 [8192, 512], P(('groups', 'dom'), 'mp'), parts along dimension 0
- edge_in_grad: float32 [3072, 512], P(('groups', 'dom'), 'mp'), parts along dimension 0
- edge_out_grad: float32 [1024, 512], P(('groups', 'dom'), 'mp'), parts along dimension 0
- edge_gain_grad: float32 [1024], P(('groups', 'mp')), parts along dimension 0
- node_in_grad: float32 [2048, 512], P(('groups', 'dom'), 'mp'), parts along dimension 0
- node_out_grad: float32 [1024, 512], P(('groups', 'dom'), 'mp'), parts along dimension 0
- node_gain_grad: float32 [1024], P(('groups', 'mp')), parts along dimension 0
There are 2 independent parts, one for each index of `groups`. A program takes and returns all parts, laid end to end along the dimension named above; an argument that names none is the same for every part. Nothing has to cross between parts.
Inputs may be any that keep to these rules, and one draw needn't show every extreme that they name: `senders`: below 128: a node of the edge's own device. Otherwise 128 + p * 32 + k names slot k that device p fills for this device, p never the edge's own device; slots that no edge names may hold any node. `receivers`: every node receives exactly 8 of its device's edges. `send_nodes`: nodes of device p, the sender.
All inputs are finite; a program needn't handle non-finite values.
Results may differ from a plain program's by a relative error of at most 0.012.
Values may be sent and summed in bfloat16 or wider, within the bound.
A program may use at most 64 MiB of HBM per device.

v0:
```python
import jax
import jax.numpy as jnp
from jax import lax
from jax.sharding import PartitionSpec as P

norm_eps = 1e-05


def shortened(value):

    def short(part):
        return part.astype(jnp.bfloat16) if part.dtype == jnp.float32 else part

    return jax.tree.map(short, value)


def silu_slope(values):
    sigma = jax.nn.sigmoid(values)
    return sigma * (1.0 + values * (1.0 - sigma))


def dot_first(left, right):
    return lax.dot_general(
        left, right, (((0,), (0,)), ((), ())), preferred_element_type=jnp.float32
    )


def dot_last(left, right):
    return lax.dot_general(
        left, right, (((1,), (1,)), ((), ())), preferred_element_type=jnp.float32
    )


def add_rows_into(index, count, values):
    table = (index[:, None] == jnp.arange(count, dtype=jnp.int32)[None, :]).astype(values.dtype)
    if values.dtype == jnp.float32:
        return lax.dot_general(
            table,
            values,
            (((0,), (0,)), ((), ())),
            precision=lax.Precision.HIGHEST,
            preferred_element_type=jnp.float32,
        )
    return dot_first(table, values)


def join_columns(values):
    return jax.tree.map(
        lambda part, own: part.astype(own.dtype),
        lax.all_gather(shortened(values), "mp", axis=1, tiled=True),
        values,
    )


def row_moments(first_term, second_term):
    return lax.psum((jnp.sum(first_term, axis=1), jnp.sum(second_term, axis=1)), "mp")


def swap_crossing(values):
    return lax.all_to_all(values, "dom", split_axis=0, concat_axis=0, tiled=True)


def reduce_grads(values):
    return (
        lax.psum_scatter(
            values[0].astype(jnp.bfloat16), "dom", scatter_dimension=0, tiled=True
        ).astype(jnp.float32),
        lax.psum_scatter(
            values[1].astype(jnp.bfloat16), "dom", scatter_dimension=0, tiled=True
        ).astype(jnp.float32),
    )


def norm_parts(values, latent_width):
    first_sum, second_sum = row_moments(values, values * values)
    center = (first_sum / latent_width)[:, None]
    spread = (second_sum / latent_width)[:, None] - center * center
    scale_inv = lax.rsqrt(spread + norm_eps)
    return ((values - center) * scale_inv, scale_inv)


def norm_back(upstream, gain_row, hatted, scale_inv, latent_width):
    weighted = upstream * gain_row
    first_sum, second_sum = row_moments(weighted, weighted * hatted)
    return scale_inv * (
        weighted
        - (first_sum / latent_width)[:, None]
        - hatted * (second_sum / latent_width)[:, None]
    )


def body(
    node_latents,
    edge_latents,
    node_cotangent,
    edge_cotangent,
    senders,
    receivers,
    send_nodes,
    edge_in_weight,
    edge_out_weight,
    edge_gain,
    node_in_weight,
    node_out_weight,
    node_gain,
):
    dom_count = lax.axis_size("dom")
    mp_count = lax.axis_size("mp")
    nodes_dev, latent_width = node_latents.shape
    edges_dev = edge_latents.shape[0]
    column_share = latent_width // mp_count
    column_start = lax.axis_index("mp") * column_share
    edge_scale = float(edges_dev * dom_count) ** (-0.5)
    node_scale = float(nodes_dev * dom_count) ** (-0.5)
    send_table = send_nodes[0].reshape(-1)
    halo_rows = swap_crossing(node_latents[send_table])
    extended = jnp.concatenate([node_latents, halo_rows], axis=0)
    edge_input = jnp.concatenate([edge_latents, extended[senders], node_latents[receivers]], axis=1)
    edge_pre = jnp.dot(edge_input, edge_in_weight, preferred_element_type=jnp.float32)
    edge_hidden = join_columns(jax.nn.silu(edge_pre).astype(jnp.bfloat16))
    edge_out = jnp.dot(edge_hidden, edge_out_weight, preferred_element_type=jnp.float32)
    edge_hat, edge_rstd = norm_parts(edge_out, latent_width)
    edge_update = (edge_hat * edge_gain).astype(jnp.bfloat16)
    aggregate = add_rows_into(receivers, nodes_dev, edge_update).astype(jnp.bfloat16)
    node_input = jnp.concatenate([node_latents, join_columns(aggregate)], axis=1)
    node_pre = jnp.dot(node_input, node_in_weight, preferred_element_type=jnp.float32)
    node_hidden = join_columns(jax.nn.silu(node_pre).astype(jnp.bfloat16))
    node_out = jnp.dot(node_hidden, node_out_weight, preferred_element_type=jnp.float32)
    node_hat, node_rstd = norm_parts(node_out, latent_width)
    out_edge_full, out_node_full = join_columns((edge_out_weight, node_out_weight))
    in_edge_full, in_node_full = join_columns((edge_in_weight, node_in_weight))
    node_cot = node_cotangent.astype(jnp.float32)
    edge_cot = edge_cotangent.astype(jnp.float32)
    node_gain_part = jnp.sum(node_cot * node_hat, axis=0) * node_scale
    node_slope = norm_back(node_cot, node_gain, node_hat, node_rstd, latent_width).astype(
        jnp.bfloat16
    )
    node_out_part = dot_first(node_hidden, node_slope) * node_scale
    node_slope_full = join_columns(node_slope)
    node_hidden_rows = lax.dynamic_slice_in_dim(out_node_full, column_start, column_share, 0)
    node_delta = (dot_last(node_slope_full, node_hidden_rows) * silu_slope(node_pre)).astype(
        jnp.bfloat16
    )
    node_in_part = dot_first(node_input, node_delta) * node_scale
    node_in_grad, node_out_grad = reduce_grads((node_in_part, node_out_part))
    node_delta_full = join_columns(node_delta)
    node_feature_rows = lax.dynamic_slice_in_dim(
        in_node_full.reshape(2, latent_width, latent_width), column_start, column_share, 1
    )
    node_back = jnp.einsum(
        "nj,bkj->bnk", node_delta_full, node_feature_rows, preferred_element_type=jnp.float32
    )
    update_grad = edge_cot + node_back[1][receivers]
    edge_gain_part = jnp.sum(update_grad * edge_hat, axis=0) * edge_scale
    edge_slope = norm_back(update_grad, edge_gain, edge_hat, edge_rstd, latent_width).astype(
        jnp.bfloat16
    )
    edge_out_part = dot_first(edge_hidden, edge_slope) * edge_scale
    edge_slope_full = join_columns(edge_slope)
    edge_hidden_rows = lax.dynamic_slice_in_dim(out_edge_full, column_start, column_share, 0)
    edge_delta = (dot_last(edge_slope_full, edge_hidden_rows) * silu_slope(edge_pre)).astype(
        jnp.bfloat16
    )
    edge_in_part = dot_first(edge_input, edge_delta) * edge_scale
    edge_delta_full = join_columns(edge_delta)
    edge_feature_rows = lax.dynamic_slice_in_dim(
        in_edge_full.reshape(3, latent_width, latent_width), column_start, column_share, 1
    )
    edge_back = jnp.einsum(
        "ej,bkj->bek", edge_delta_full, edge_feature_rows, preferred_element_type=jnp.float32
    )
    edge_grad = (edge_cot + edge_back[0]).astype(jnp.bfloat16)
    sender_sums = add_rows_into(senders, nodes_dev + send_table.shape[0], edge_back[1])
    returned_rows = swap_crossing(sender_sums[nodes_dev:].astype(jnp.bfloat16))
    returned = add_rows_into(send_table, nodes_dev, returned_rows)
    receiver_sums = add_rows_into(receivers, nodes_dev, edge_back[2])
    node_grad = (
        node_cot + node_back[0] + receiver_sums + sender_sums[:nodes_dev] + returned
    ).astype(jnp.bfloat16)
    edge_in_grad, edge_out_grad = reduce_grads((edge_in_part, edge_out_part))
    edge_gain_grad, node_gain_grad = lax.psum((edge_gain_part, node_gain_part), "dom")
    return (
        node_grad,
        edge_grad,
        edge_in_grad,
        edge_out_grad,
        edge_gain_grad,
        node_in_grad,
        node_out_grad,
        node_gain_grad,
    )


def solution(mesh):
    in_specs = (
        P(("groups", "dom"), None),
        P(("groups", "dom"), None),
        P(("groups", "dom"), "mp"),
        P(("groups", "dom"), "mp"),
        P("dom"),
        P("dom"),
        P("dom", None, None),
        P(None, "mp"),
        P(None, "mp"),
        P("mp"),
        P(None, "mp"),
        P(None, "mp"),
        P("mp"),
    )
    out_specs = (
        P(("groups", "dom"), "mp"),
        P(("groups", "dom"), "mp"),
        P(("groups", "dom"), "mp"),
        P(("groups", "dom"), "mp"),
        P(("groups", "mp")),
        P(("groups", "dom"), "mp"),
        P(("groups", "dom"), "mp"),
        P(("groups", "mp")),
    )
    return jax.shard_map(body, mesh=mesh, in_specs=in_specs, out_specs=out_specs, check_vma=False)
```

profile of v0, /device:TPU:0, one launch (start us, length us, event | category | flops | bytes accessed | tf_op | source)
XLA Modules:
  0.0 268.8 jit_solution(13357317420196492549)
XLA Ops:
  7.2 0.8 reshape_squeeze.3
  8.7 2.4 gather_fusion
  11.1 6.3 %all-to-all-start = ((bf16[4,32,512]{2,1,0:T(8,128)(2,1)}), bf16[4,32,512]{2,1,0:T(8,128)(2,1)S(1)}, u32[]{:S(2)}, u32[]{:S(2)}) async-start(bf16[4,32,512]{2,1,0:T(8,128)(2,1)} %bitcast.2), calls=%async_computation | async-start | bytes 262144 | tf_op jit(solution)/shard_map/all_to_all | solution.py:60
  17.5 4.0 %gather_fusion.2 = bf16[1024,512]{1,0:T(8,128)(2,1)S(1)} fusion(bf16[128,512]{1,0:T(8,128)(2,1)S(1)} %copy-done, s32[1024]{0:T(1024)S(1)} %get-tuple-element.46), kind=kCustom, calls=%fused_computation.2 | custom fusion | bytes 2101248 | tf_op jit(solution)/shard_map/gather | solution.py:118
  21.5 1.1 constant_dynamic-update-slice_fusion.2
  22.6 1.0 all-to-all-done
  23.5 4.0 %gather_fusion.1 = bf16[1024,512]{1,0:T(8,128)(2,1)S(1)} fusion(bf16[256,512]{1,0:T(8,128)(2,1)S(1)} %pad_maximum_fusion, s32[1024]{0:T(1024)S(1)} %fusion.35), kind=kCustom, calls=%fused_computation.1 | custom fusion | bytes 2101248 | tf_op jit(solution)/shard_map/gather | solution.py:118
  27.5 1.1 constant_dynamic-update-slice_fusion.1
  28.7 1.1 constant_dynamic-update-slice_fusion
  29.8 3.8 %multiply_convert_fusion.2 = (bf16[1024,128]{1,0:T(8,128)(2,1)}, f32[1024,128]{1,0:T(8,128)}) fusion(bf16[1024,1536]{1,0:T(8,128)(2,1)} %constant_dynamic-update-slice_fusion, bf16[1536,128]{1,0:T(8,128)(2,1)S(1)} %copy-done.6), kind=kOutput, calls=%fused_computation.40 | convolution fusion | flops 403308544 | bytes 4325376 | tf_op jit(solution)/shard_map/dot_general | solution.py:119
  34.6 7.2 %all_gather.38 = bf16[512,512]{1,0:T(8,128)(2,1)S(1)} all-gather(bf16[512,128]{1,0:T(8,128)(2,1)S(1)} %copy-done.3), channel_id=1, replica_groups=mesh['groups'=2,'dom'=4,'mp'=4] {'mp'}, dimensions={1}, use_global_device_ids=true | all-gather | bytes 655360 | tf_op jit(solution)/shard_map/all_gather | solution.py:50
  42.0 9.2 %all-gather.8.cloned.1.call-done = bf16[1024,512]{1,0:T(8,128)(2,1)} async-done(((bf16[1024,128]{1,0:T(8,128)(2,1)}), bf16[1024,512]{1,0:T(8,128)(2,1)}) %all-gather.8.cloned.1.call-update) | async-done | bytes 1048592 | tf_op jit(solution)/shard_map/all_gather | solution.py:50
  51.2 1.7 fusion.42
  52.9 6.0 %all-reduce.3 = (f32[1024]{0:T(1024)S(1)}, f32[1024]{0:T(1024)S(1)}) all-reduce(f32[1024]{0:T(1024)S(1)} %get-tuple-element.20, f32[1024]{0:T(1024)S(1)} %get-tuple-element.19), channel_id=1, replica_groups=mesh['groups'=2,'dom'=4,'mp'=4] {'mp'}, use_global_device_ids=true, to_apply=%region_3.4 | all-reduce | flops 2048 | bytes 16384 | tf_op jit(solution)/shard_map/psum | solution.py:56
  59.4 5.5 %all_gather.35 = bf16[128,512]{1,0:T(8,128)(2,1)S(1)} all-gather(bf16[128,128]{1,0:T(8,128)(2,1)S(1)} %convolution_convert_fusion), channel_id=1, replica_groups=mesh['groups'=2,'dom'=4,'mp'=4] {'mp'}, dimensions={1}, use_global_device_ids=true | all-gather | bytes 163840 | tf_op jit(solution)/shard_map/all_gather | solution.py:50
  65.1 6.0 %all_gather.36 = bf16[128,512]{1,0:T(8,128)(2,1)S(1)} all-gather(bf16[128,128]{1,0:T(8,128)(2,1)S(1)} %get-tuple-element.43), channel_id=1, replica_groups=mesh['groups'=2,'dom'=4,'mp'=4] {'mp'}, dimensions={1}, use_global_device_ids=true | all-gather | bytes 163840 | tf_op jit(solution)/shard_map/all_gather | solution.py:50
  71.3 7.3 %all-reduce.2 = (f32[128]{0:T(128)S(1)}, f32[128]{0:T(128)S(1)}) all-reduce(f32[128]{0:T(128)S(1)} %get-tuple-element.24, f32[128]{0:T(128)S(1)} %get-tuple-element.23), channel_id=1, replica_groups=mesh['groups'=2,'dom'=4,'mp'=4] {'mp'}, use_global_device_ids=true, to_apply=%region_7.8 | all-reduce | flops 256 | bytes 2048 | tf_op jit(solution)/shard_map/psum | solution.py:56
  78.8 5.8 %all-reduce.1 = (f32[128]{0:T(128)S(1)}, f32[128]{0:T(128)S(1)}) all-reduce(f32[128]{0:T(128)S(1)} %get-tuple-element.22, f32[128]{0:T(128)S(1)} %get-tuple-element.25), channel_id=1, replica_groups=mesh['groups'=2,'dom'=4,'mp'=4] {'mp'}, use_global_device_ids=true, to_apply=%region_11.12 | all-reduce | flops 256 | bytes 2048 | tf_op jit(solution)/shard_map/psum | solution.py:56
  84.7 5.4 %all_gather.37 = bf16[128,512]{0,1:T(8,128)(2,1)S(1)} all-gather(bf16[128,128]{0,1:T(8,128)(2,1)S(1)} %fusion.31), channel_id=1, replica_groups=mesh['groups'=2,'dom'=4,'mp'=4] {'mp'}, dimensions={1}, use_global_device_ids=true | all-gather | bytes 163840 | tf_op jit(solution)/shard_map/all_gather | solution.py:50
  90.3 5.4 %all_gather.39 = bf16[128,512]{1,0:T(8,128)(2,1)S(1)} all-gather(bf16[128,128]{1,0:T(8,128)(2,1)S(1)} %fusion.6), channel_id=1, replica_groups=mesh['groups'=2,'dom'=4,'mp'=4] {'mp'}, dimensions={1}, use_global_device_ids=true | all-gather | bytes 163840 | tf_op jit(solution)/shard_map/all_gather | solution.py:50
  95.8 1.2 convolution_bitcast_fusion.1
  97.1 2.8 %gather_fusion.3 = f32[1024,128]{1,0:T(8,128)S(1)} fusion(f32[128,128]{1,0:T(8,128)S(1)} %copy.23, s32[1024]{0:T(1024)S(1)} %get-tuple-element.46), kind=kCustom, calls=%fused_computation.3 | custom fusion | bytes 1052672 | tf_op jit(solution)/shard_map/gather | solution.py:153
  100.3 6.1 %all-reduce = (f32[1024]{0:T(1024)S(1)}, f32[1024]{0:T(1024)S(1)}) all-reduce(f32[1024]{0:T(1024)S(1)} %get-tuple-element.17, f32[1024]{0:T(1024)S(1)} %get-tuple-element.18), channel_id=1, replica_groups=mesh['groups'=2,'dom'=4,'mp'=4] {'mp'}, use_global_device_ids=true, to_apply=%region_15.16 | all-reduce | flops 2048 | bytes 16384 | tf_op jit(solution)/shard_map/psum | solution.py:56
  106.5 0.9 multiply_convert_fusion
  107.4 0.9 fusion.3
  108.4 2.1 fusion.4
  110.6 7.3 %all_gather.42 = bf16[512,512]{1,0:T(8,128)(2,1)S(1)} all-gather(bf16[512,128]{1,0:T(8,128)(2,1)S(1)} %copy-done.5), channel_id=1, replica_groups=mesh['groups'=2,'dom'=4,'mp'=4] {'mp'}, dimensions={1}, use_global_device_ids=true | all-gather | bytes 655360 | tf_op jit(solution)/shard_map/all_gather | solution.py:50
  117.9 1.0 fusion.1
  118.9 6.4 %all-gather.12.cloned.1.call-done = bf16[1024,512]{0,1:T(8,128)(2,1)} async-done(((bf16[1024,128]{0,1:T(8,128)(2,1)}), bf16[1024,512]{0,1:T(8,128)(2,1)}) %all-gather.12.cloned.1.call-update) | async-done | bytes 1048592 | tf_op jit(solution)/shard_map/all_gather | solution.py:50
  125.4 1.7 fusion.2
  127.1 3.8 %fusion = bf16[1536,128]{1,0:T(8,128)(2,1)} fusion(bf16[1024,1536]{1,0:T(8,128)(2,1)} %constant_dynamic-update-slice_fusion, bf16[1024,128]{1,0:T(8,128)(2,1)S(1)} %fusion.2), kind=kOutput, calls=%fused_computation.5 | convolution fusion | flops 403046400 | bytes 3801088 | tf_op jit(solution)/shard_map/dot_general | solution.py:23
  132.5 12.3 %all-reduce.4 = (f32[128]{0:T(128)}, f32[128]{0:T(128)}) all-reduce(f32[128]{0:T(128)S(1)} %broadcast_multiply_fusion.4, f32[128]{0:T(128)S(1)} %broadcast_multiply_fusion.3), channel_id=1, replica_groups=mesh['groups'=2,'dom'=4,'mp'=4] {'dom'}, use_global_device_ids=true, to_apply=%region_19.20 | all-reduce | flops 256 | bytes 2048 | tf_op jit(solution)/shard_map/psum | solution.py:181
  144.7 2.6 reduce-scatter.11.cloned.1.call-done
  147.3 1.4 convert_element_type.84
  148.7 18.7 %reduce-scatter.7.cloned.1.call-done = bf16[128,128]{1,0:T(8,128)(2,1)} async-done(((bf16[512,128]{1,0:T(8,128)(2,1)}), bf16[128,128]{1,0:T(8,128)(2,1)}) %reduce-scatter.7.cloned.1.call-update) | async-done | bytes 32784 | tf_op jit(solution)/shard_map/reduce_scatter | solution.py:68
  167.4 1.4 convert_element_type.80
  168.8 18.6 %reduce-scatter.9.cloned.1.call-done = bf16[256,128]{1,0:T(8,128)(2,1)} async-done(((bf16[1024,128]{1,0:T(8,128)(2,1)}), bf16[256,128]{1,0:T(8,128)(2,1)}) %reduce-scatter.9.cloned.1.call-update) | async-done | bytes 65552 | tf_op jit(solution)/shard_map/reduce_scatter | solution.py:65
  187.4 1.5 convert_element_type.82
  188.9 19.7 %reduce-scatter.5.cloned.1.call-done = bf16[384,128]{1,0:T(8,128)(2,1)} async-done(((bf16[1536,128]{1,0:T(8,128)(2,1)}), bf16[384,128]{1,0:T(8,128)(2,1)}) %reduce-scatter.5.cloned.1.call-update) | async-done | bytes 98320 | tf_op jit(solution)/shard_map/reduce_scatter | solution.py:65
  208.7 1.6 convert_element_type.78
  210.3 18.1 %all-gather.10.cloned.1.call-done = bf16[1536,512]{1,0:T(8,128)(2,1)} async-done(((bf16[1536,128]{1,0:T(8,128)(2,1)}), bf16[1536,512]{1,0:T(8,128)(2,1)}) %all-gather.10.cloned.1.call-update) | async-done | bytes 1572880 | tf_op jit(solution)/shard_map/all_gather | solution.py:50
  228.4 19.0 %all-gather.14.cloned.1.call-done = bf16[1024,512]{1,0:T(8,128)(2,1)} async-done(((bf16[1024,128]{1,0:T(8,128)(2,1)}), bf16[1024,512]{1,0:T(8,128)(2,1)}) %all-gather.14.cloned.1.call-update) | async-done | bytes 1048592 | tf_op jit(solution)/shard_map/all_gather | solution.py:50
  247.4 1.9 convolution_bitcast_fusion
  249.4 0.9 fusion.11
  251.0 4.6 %all-to-all-start.1 = ((bf16[4,32,128]{2,1,0:T(8,128)(2,1)}), bf16[4,32,128]{2,1,0:T(8,128)(2,1)S(1)}, u32[]{:S(2)}, u32[]{:S(2)}) async-start(bf16[4,32,128]{2,1,0:T(8,128)(2,1)} %bitcast.13), calls=%async_computation.1 | async-start | bytes 65536 | tf_op jit(solution)/shard_map/all_to_all | solution.py:60
  256.2 0.8 copy.29
  257.0 4.3 %all-to-all-done.1 = bf16[4,32,128]{2,1,0:T(8,128)(2,1)S(1)} async-done(((bf16[4,32,128]{2,1,0:T(8,128)(2,1)}), bf16[4,32,128]{2,1,0:T(8,128)(2,1)S(1)}, u32[]{:S(2)}, u32[]{:S(2)}) %all-to-all-start.1) | async-done | bytes 32800 | tf_op jit(solution)/shard_map/all_to_all | solution.py:60
  261.6 0.7 copy.28
  (86 shorter events, 7.1 us)
Async XLA Ops:
  7.2 10.3 %copy-start = (bf16[128,512]{1,0:T(8,128)(2,1)S(1)}, bf16[128,512]{1,0:T(8,128)(2,1)}, u32[]{:S(2)}) copy-start(bf16[128,512]{1,0:T(8,128)(2,1)} %param.13) | copy-start | bytes 393220
  11.1 12.4 %all-to-all-start = ((bf16[4,32,512]{2,1,0:T(8,128)(2,1)}), bf16[4,32,512]{2,1,0:T(8,128)(2,1)S(1)}, u32[]{:S(2)}, u32[]{:S(2)}) async-start(bf16[4,32,512]{2,1,0:T(8,128)(2,1)} %bitcast.2), calls=%async_computation | async-start | bytes 262144 | tf_op jit(solution)/shard_map/all_to_all | solution.py:60
  17.4 33.7 %all-gather.8.cloned.1.call-start = ((), (), s32[]{:S(2)}) async-start(), calls=%async_computation.7 | async-start | bytes 1310720 | tf_op jit(solution)/shard_map/all_gather | solution.py:50
  17.5 4.0 %copy-start.2 = (bf16[1024,512]{1,0:T(8,128)(2,1)S(1)}, bf16[1024,512]{1,0:T(8,128)(2,1)}, u32[]{:S(2)}) copy-start(bf16[1024,512]{1,0:T(8,128)(2,1)} %param.14) | copy-start | bytes 3145732
  17.5 5.1 %copy-start.12 = (s32[1024]{0:T(1024)S(1)}, s32[1024]{0:T(1024)}, u32[]{:S(2)}) copy-start(s32[1024]{0:T(1024)} %param.17) | copy-start | bytes 12292
  27.5 2.3 copy-start.6
  29.8 4.7 %copy-start.10 = (bf16[128,128]{1,0:T(8,128)(2,1)S(1)}, bf16[128,128]{1,0:T(8,128)(2,1)}, u32[]{:S(2)}) copy-start(bf16[128,128]{1,0:T(8,128)(2,1)} %param.15) | copy-start | bytes 98308
  29.8 4.8 %copy-start.3 = (bf16[512,128]{1,0:T(8,128)(2,1)S(1)}, bf16[512,128]{1,0:T(8,128)(2,1)}, u32[]{:S(2)}) copy-start(bf16[512,128]{1,0:T(8,128)(2,1)} %param.24) | copy-start | bytes 393220
  29.8 12.0 %copy-start.7 = (bf16[1024,128]{1,0:T(8,128)(2,1)S(1)}, bf16[1024,128]{1,0:T(8,128)(2,1)}, u32[]{:S(2)}) copy-start(bf16[1024,128]{1,0:T(8,128)(2,1)} %param.16) | copy-start | bytes 786436
  29.8 21.4 %copy-start.4 = (bf16[512,128]{1,0:T(8,128)(2,1)S(1)}, bf16[512,128]{1,0:T(8,128)(2,1)}, u32[]{:S(2)}) copy-start(bf16[512,128]{1,0:T(8,128)(2,1)} %param.21) | copy-start | bytes 393220
  33.6 25.3 %copy-start.11 = (s32[1024]{0:T(1024)S(1)}, s32[1024]{0:T(1024)}, u32[]{:S(2)}) copy-start(s32[1024]{0:T(1024)} %param.18) | copy-start | bytes 12292
  33.6 25.3 %copy-start.15 = (f32[128]{0:T(128)S(1)}, f32[128]{0:T(128)}, u32[]{:S(2)}) copy-start(f32[128]{0:T(128)} %param.22) | copy-start | bytes 1540
  33.6 31.3 %copy-start.8 = (bf16[1024,128]{1,0:T(8,128)(2,1)S(1)}, bf16[1024,128]{1,0:T(8,128)(2,1)}, u32[]{:S(2)}) copy-start(bf16[1024,128]{1,0:T(8,128)(2,1)} %param.23) | copy-start | bytes 786436
  33.6 45.1 %copy-start.14 = (f32[128]{0:T(128)S(1)}, f32[128]{0:T(128)}, u32[]{:S(2)}) copy-start(f32[128]{0:T(128)} %param.25) | copy-start | bytes 1540
  33.6 62.2 %all-gather.6.cloned.1.call-start = ((), (), s32[]{:S(2)}) async-start(), calls=%async_computation.6 | async-start | bytes 1310720 | tf_op jit(solution)/shard_map/all_gather | solution.py:50
  34.4 91.0 %all-gather.12.cloned.1.call-start = ((), (), s32[]{:S(2)}) async-start(), calls=%async_computation.9 | async-start | bytes 1310720 | tf_op jit(solution)/shard_map/all_gather | solution.py:50
  99.9 8.5 %copy-start.1 = (bf16[1024,512]{1,0:T(8,128)(2,1)S(1)}, bf16[1024,512]{1,0:T(8,128)(2,1)}, u32[]{:S(2)}) copy-start(bf16[1024,512]{1,0:T(8,128)(2,1)} %all-gather.8.cloned.1.call-done) | copy-start | bytes 3145732
  100.1 10.4 %copy-start.5 = (bf16[512,128]{1,0:T(8,128)(2,1)S(1)}, bf16[512,128]{1,0:T(8,128)(2,1)}, u32[]{:S(2)}) copy-start(bf16[512,128]{1,0:T(8,128)(2,1)} %param.21) | copy-start | bytes 393220
  107.4 18.0 %copy-start.16 = (f32[1024,128]{1,0:T(8,128)S(1)}, f32[1024,128]{1,0:T(8,128)}, u32[]{:S(2)}) copy-start(f32[1024,128]{1,0:T(8,128)} %get-tuple-element.41) | copy-start | bytes 1572868
  107.4 39.9 %reduce-scatter.11.cloned.1.call-start = ((), (), s32[]{:S(2)}) async-start(), calls=%async_computation.14 | async-start | bytes 163840 | tf_op jit(solution)/shard_map/reduce_scatter | solution.py:68
  108.3 59.1 %reduce-scatter.7.cloned.1.call-start = ((), (), s32[]{:S(2)}) async-start(), calls=%async_computation.12 | async-start | bytes 163840 | tf_op jit(solution)/shard_map/reduce_scatter | solution.py:68
  110.5 76.9 %reduce-scatter.9.cloned.1.call-start = ((), (), s32[]{:S(2)}) async-start(), calls=%async_computation.13 | async-start | bytes 327680 | tf_op jit(solution)/shard_map/reduce_scatter | solution.py:65
  118.9 89.8 %reduce-scatter.5.cloned.1.call-start = ((), (), s32[]{:S(2)}) async-start(), calls=%async_computation.11 | async-start | bytes 491520 | tf_op jit(solution)/shard_map/reduce_scatter | solution.py:65
  127.1 4.6 %copy-start.9 = (bf16[1024,128]{1,0:T(8,128)(2,1)}, bf16[1024,128]{1,0:T(8,128)(2,1)S(1)}, u32[]{:S(2)}) copy-start(bf16[1024,128]{1,0:T(8,128)(2,1)S(1)} %fusion.2) | copy-start | bytes 786436
  127.1 5.3 %copy-start.13 = (s32[1,4,32]{2,1,0:T(4,128)S(1)}, s32[1,4,32]{2,1,0:T(4,128)}, u32[]{:S(2)}) copy-start(s32[1,4,32]{2,1,0:T(4,128)} %param.19) | copy-start | bytes 1540
  130.9 97.5 %all-gather.10.cloned.1.call-start = ((), (), s32[]{:S(2)}) async-start(), calls=%async_computation.8 | async-start | bytes 1966080 | tf_op jit(solution)/shard_map/all_gather | solution.py:50
  131.6 115.8 %all-gather.14.cloned.1.call-start = ((), (), s32[]{:S(2)}) async-start(), calls=%async_computation.10 | async-start | bytes 1310720 | tf_op jit(solution)/shard_map/all_gather | solution.py:50
  251.0 10.3 %all-to-all-start.1 = ((bf16[4,32,128]{2,1,0:T(8,128)(2,1)}), bf16[4,32,128]{2,1,0:T(8,128)(2,1)S(1)}, u32[]{:S(2)}, u32[]{:S(2)}) async-start(bf16[4,32,128]{2,1,0:T(8,128)(2,1)} %bitcast.13), calls=%async_computation.1 | async-start | bytes 65536 | tf_op jit(solution)/shard_map/all_to_all | solution.py:60
Sparse Core Ops, SparseCore 0:
  33.8 17.3 all-gather.7
  52.7 17.5 all-gather.5
  107.5 17.7 all-gather.11
  128.0 19.2 reduce-scatter.10
  150.1 17.3 reduce-scatter.6
  169.6 17.8 reduce-scatter.8
  189.8 18.8 reduce-scatter.4
  210.2 18.1 all-gather.9
  230.5 16.8 all-gather.13
where the time goes:
time: 270 us; the launch traced here: 269 us
  waiting for transfers between devices  120 us (44%)
  blocking collectives  74.3 us (28%)
  matrix products  20.8 us (8%)
  local copies, waits for them, and re-layouts  20.3 us (8%)
  between operations  14.2 us (5%)
  starting transfers between devices  11.3 us (4%)
  other arithmetic  8.02 us (3%)
    all_gather x5, waiting for transfers between devices, join_columns(): lax.all_gather(shortened(values), 'mp', axis=1, tiled=True)  52.8 us
    reduce_scatter x2, waiting for transfers between devices, reduce_grads(): lax.psum_scatter(values[0].astype(jnp.bfloat16), 'dom', scatter_dimension...  38.3 us
    all_gather x6, blocking collectives, join_columns(): lax.all_gather(shortened(values), 'mp', axis=1, tiled=True)  36.8 us
    psum x4, blocking collectives, row_moments(): lax.psum((jnp.sum(first_term, axis=1), jnp.sum(second_term, axis=1)), 'mp')  25.2 us
    reduce_scatter x2, waiting for transfers between devices, reduce_grads(): lax.psum_scatter(values[1].astype(jnp.bfloat16), 'dom', scatter_dimension...  21.3 us
    psum x1, blocking collectives, body(): lax.psum((edge_gain_part, node_gain_part), 'dom')  12.3 us
    all_to_all x2, starting transfers between devices, swap_crossing(): lax.all_to_all(values, 'dom', split_axis=0, concat_axis=0, tiled=True)  10.9 us
    dot_general x6, matrix products, dot_first(): lax.dot_general(left, right, (((0,), (0,)), ((), ())), preferred_element_...  8.36 us
  transfers between devices with their start and end apart: 11, of which 10 were waited for; matrix products, arithmetic and copies ran while one was open for 9% of the time, Pallas kernels for 0%

commit v1 on v0

--- a/solution.py
+++ b/solution.py
@@ -1,6 +1,10 @@
+import functools
+
 import jax
 import jax.numpy as jnp
 from jax import lax
+from jax.experimental import pallas as pl
+from jax.experimental.pallas import tpu as pltpu
 from jax.sharding import PartitionSpec as P
 
 norm_eps = 1e-05
@@ -191,6 +195,523 @@
     )
 
 
+def dot_plain(left, right):
+    return jnp.dot(left, right, preferred_element_type=jnp.float32)
+
+
+def two_terms(values):
+    high = values.astype(jnp.bfloat16)
+    low = (values - high.astype(jnp.float32)).astype(jnp.bfloat16)
+    return jnp.concatenate([high, low], axis=1)
+
+
+def join_terms(values):
+    half = values.shape[1] // 2
+    return values[:, :half] + values[:, half:]
+
+
+def repeat_rows(values, times):
+    rows, columns = values.shape
+    return jnp.broadcast_to(values[:, None, :], (rows, times, columns)).reshape(
+        rows * times, columns
+    )
+
+
+def sum_rows(values, times):
+    rows, columns = values.shape
+    return jnp.sum(values.reshape(rows // times, times, columns), axis=1)
+
+
+def local_norm(values):
+    center = jnp.mean(values, axis=1, keepdims=True)
+    spread = jnp.mean(values * values, axis=1, keepdims=True) - center * center
+    scale_inv = lax.rsqrt(spread + norm_eps)
+    return (values - center) * scale_inv, scale_inv
+
+
+def local_norm_back(upstream, gain_row, hatted, scale_inv):
+    weighted = upstream * gain_row
+    first_mean = jnp.mean(weighted, axis=1, keepdims=True)
+    second_mean = jnp.mean(weighted * hatted, axis=1, keepdims=True)
+    return scale_inv * (weighted - first_mean - hatted * second_mean)
+
+
+def fused_kernel(
+    dom,
+    mp,
+    degree,
+    nodes,
+    edges,
+    node_cot,
+    edge_cot,
+    senders,
+    receivers,
+    table,
+    w_in,
+    w_out,
+    e_gain,
+    nw_in,
+    nw_out,
+    n_gain,
+    node_grad,
+    edge_grad,
+    edge_in_grad,
+    edge_out_grad,
+    edge_gain_grad,
+    node_in_grad,
+    node_out_grad,
+    node_gain_grad,
+    halo_send,
+    extended,
+    w_out_all,
+    nw_in_all,
+    nw_out_all,
+    w_in_rows,
+    e_gain_all,
+    n_gain_all,
+    perm,
+    edges_sorted,
+    cot_sorted,
+    grad_sorted,
+    sender_hot,
+    pre_cols,
+    pre_rows,
+    cot_rows,
+    ncot_rows,
+    agg_all,
+    nhid_all,
+    ndelta_all,
+    nslope_own,
+    nslope_cols,
+    delta_all,
+    gain_part,
+    gain_recv,
+    gain_sum,
+    gain_dom,
+    eo_part,
+    eo_recv,
+    eo_send,
+    eo_dom,
+    ei_send,
+    ei_dom,
+    no_send,
+    no_dom,
+    ni_send,
+    ni_dom,
+    cross_send,
+    cross_recv,
+    back_terms,
+    receiver_back,
+    mp_send_sem,
+    mp_recv_sem,
+    dom_send_sem,
+    dom_recv_sem,
+):
+    f32, bf16 = jnp.float32, jnp.bfloat16
+    node_count, width = nodes.shape
+    edge_count = edges.shape[0]
+    share = width // mp
+    my_nodes, my_edges = node_count // mp, edge_count // mp
+    slots = table.shape[1]
+    cap = slots // dom
+    edge_scale = float(edge_count * dom) ** (-0.5)
+    node_scale = float(node_count * dom) ** (-0.5)
+    me_m, me_d = lax.axis_index("mp"), lax.axis_index("dom")
+
+    def rows(index, size):
+        return pl.ds(pl.multiple_of(index * size, size), size)
+
+    mp_to = [lax.rem(me_m + k, mp) for k in range(1, mp)]
+    mp_from = [lax.rem(me_m + mp - k, mp) for k in range(1, mp)]
+    dom_to = [lax.rem(me_d + k, dom) for k in range(1, dom)]
+    dom_from = [lax.rem(me_d + dom - k, dom) for k in range(1, dom)]
+    started = []
+
+    def push(axis, kind, peers, source, target):
+        send, recv = (
+            (mp_send_sem, mp_recv_sem) if axis == "mp" else (dom_send_sem, dom_recv_sem)
+        )
+        copies = []
+        for k, peer in enumerate(peers):
+            copy = pltpu.make_async_remote_copy(
+                src_ref=source(peer),
+                dst_ref=target,
+                send_sem=send.at[kind, k],
+                recv_sem=recv.at[kind, k],
+                device_id={axis: peer},
+                device_id_type=pl.DeviceIdType.MESH,
+            )
+            copy.start()
+            copies.append(copy)
+        started.extend(copies)
+        return copies
+
+    def arrived(copies):
+        for copy in copies:
+            copy.wait_recv()
+
+    barrier = pltpu.get_barrier_semaphore()
+    for axis, peers in (("mp", mp_to), ("dom", dom_to)):
+        for peer in peers:
+            pl.semaphore_signal(
+                barrier, inc=1, device_id={axis: peer}, device_id_type=pl.DeviceIdType.MESH
+            )
+
+    table_hot = (
+        lax.broadcasted_iota(jnp.int32, (node_count, slots), 0) == table[...]
+    ).astype(bf16)
+    halo_send[...] = dot_first(table_hot, nodes[...]).astype(bf16)
+    extended[pl.ds(0, node_count), :] = nodes[...]
+    extended[pl.ds(pl.multiple_of(node_count + me_d * cap, cap), cap), :] = jnp.zeros(
+        (cap, width), bf16
+    )
+    pl.semaphore_wait(barrier, mp + dom - 2)
+
+    halo = push(
+        "dom",
+        0,
+        dom_to,
+        lambda peer: halo_send.at[rows(peer, cap), :],
+        extended.at[pl.ds(pl.multiple_of(node_count + me_d * cap, cap), cap), :],
+    )
+    own_cols = rows(me_m, share)
+    w_out_in = push("mp", 0, mp_to, lambda peer: w_out, w_out_all.at[:, own_cols])
+    gain_in = push("mp", 1, mp_to, lambda peer: e_gain, e_gain_all.at[:, own_cols])
+    ngain_in = push("mp", 2, mp_to, lambda peer: n_gain, n_gain_all.at[:, own_cols])
+    ncot_in = push(
+        "mp", 3, mp_to, lambda peer: node_cot.at[rows(peer, my_nodes), :], ncot_rows.at[:, own_cols]
+    )
+    w_out_all[:, own_cols] = w_out[...]
+    e_gain_all[:, own_cols] = e_gain[...]
+    n_gain_all[:, own_cols] = n_gain[...]
+    ncot_rows[:, own_cols] = node_cot[rows(me_m, my_nodes), :]
+    nw_in_all[:, own_cols] = nw_in[...]
+    nw_out_all[:, own_cols] = nw_out[...]
+    w_in_rows[:, :, own_cols] = w_in[:, rows(me_m, share), :]
+
+    lane = 128
+    before = (
+        lax.broadcasted_iota(jnp.int32, (lane, lane), 0)
+        < lax.broadcasted_iota(jnp.int32, (lane, lane), 1)
+    ).astype(bf16)
+    offset = jnp.zeros((node_count, 1), f32)
+    places = []
+    for start in range(0, edge_count, lane):
+        received = receivers[:, start : start + lane]
+        hot = lax.broadcasted_iota(jnp.int32, (node_count, lane), 0) == received
+        hot32 = hot.astype(f32)
+        earlier = dot_plain(hot32.astype(bf16), before) + offset
+        rank = jnp.sum(hot32 * earlier, axis=0, keepdims=True)
+        places.append(received * degree + rank.astype(jnp.int32))
+        offset = offset + jnp.sum(hot32, axis=1, keepdims=True)
+    place = jnp.concatenate(places, axis=1)
+    sender_cols = (
+        lax.broadcasted_iota(jnp.int32, (node_count + slots, edge_count), 0) == senders[...]
+    ).astype(bf16)
+    receiver_pre = dot_plain(nodes[...], w_in[2])
+    for part in range(mp):
+        block = pl.ds(part * my_edges, my_edges)
+        hot = (
+            lax.broadcasted_iota(jnp.int32, (my_edges, edge_count), 0) + part * my_edges == place
+        ).astype(bf16)
+        perm[block, :] = hot
+        edges_sorted[block, :] = dot_plain(hot, edges[...]).astype(bf16)
+        cot_sorted[block, :] = dot_plain(hot, edge_cot[...]).astype(bf16)
+        sender_hot[block, :] = dot_last(hot, sender_cols).astype(bf16)
+    arrived(halo)
+    sender_pre = two_terms(dot_plain(extended[...], w_in[1]))
+    for part in range(mp):
+        block = pl.ds(part * my_edges, my_edges)
+        local = dot_plain(edges_sorted[block, :], w_in[0])
+        local = local + repeat_rows(
+            receiver_pre[part * my_nodes : (part + 1) * my_nodes], degree
+        )
+        local = local + join_terms(dot_plain(sender_hot[block, :], sender_pre))
+        pre_cols[block, :] = local.astype(bf16)
+    pre_in = push(
+        "mp", 4, mp_to, lambda peer: pre_cols.at[rows(peer, my_edges), :], pre_rows.at[:, own_cols]
+    )
+    nw_in_in = push("mp", 6, mp_to, lambda peer: nw_in, nw_in_all.at[:, own_cols])
+    nw_out_in = push("mp", 7, mp_to, lambda peer: nw_out, nw_out_all.at[:, own_cols])
+    cot_in = push(
+        "mp", 5, mp_to, lambda peer: cot_sorted.at[rows(peer, my_edges), :], cot_rows.at[:, own_cols]
+    )
+    w_in_in = push(
+        "mp", 8, mp_to, lambda peer: w_in.at[:, rows(peer, share), :], w_in_rows.at[:, :, own_cols]
+    )
+    pre_rows[:, own_cols] = pre_cols[rows(me_m, my_edges), :]
+    cot_rows[:, own_cols] = cot_sorted[rows(me_m, my_edges), :]
+
+    arrived(pre_in)
+    edge_pre = pre_rows[...].astype(f32)
+    edge_hidden = (edge_pre * jax.nn.sigmoid(edge_pre)).astype(bf16)
+    arrived(w_out_in)
+    edge_out = dot_plain(edge_hidden, w_out_all[...])
+    edge_hat, edge_rstd = local_norm(edge_out)
+    arrived(gain_in)
+    edge_update = (edge_hat * e_gain_all[...]).astype(bf16).astype(f32)
+    own_rows = rows(me_m, my_nodes)
+    aggregate = sum_rows(edge_update, degree).astype(bf16)
+    agg_all[own_rows, :] = aggregate
+    agg_in = push(
+        "mp", 9, mp_to, lambda peer: agg_all.at[own_rows, :], agg_all.at[own_rows, :]
+    )
+    arrived(nw_in_in)
+    node_pre = dot_plain(nodes[own_rows, :], nw_in_all[pl.ds(0, width), :]) + dot_plain(
+        aggregate, nw_in_all[pl.ds(width, width), :]
+    )
+    node_hidden = (node_pre * jax.nn.sigmoid(node_pre)).astype(bf16)
+    nhid_all[own_rows, :] = node_hidden
+    nhid_in = push(
+        "mp", 10, mp_to, lambda peer: nhid_all.at[own_rows, :], nhid_all.at[own_rows, :]
+    )
+    arrived(nw_out_in)
+    node_hat, node_rstd = local_norm(dot_plain(node_hidden, nw_out_all[...]))
+    arrived(ncot_in)
+    arrived(ngain_in)
+    ncot = ncot_rows[...].astype(f32)
+    gain_part[...] = jnp.zeros_like(gain_part)
+    gain_part[0:1, :] = jnp.sum(ncot * node_hat, axis=0, keepdims=True) * node_scale
+    node_slope = local_norm_back(ncot, n_gain_all[...], node_hat, node_rstd).astype(bf16)
+    nslope_own[...] = node_slope
+    nslope_in = push(
+        "mp", 11, mp_to, lambda peer: nslope_own.at[:, rows(peer, share)], nslope_cols.at[own_rows, :]
+    )
+    nslope_cols[own_rows, :] = nslope_own[:, own_cols]
+    node_delta = (dot_last(node_slope, nw_out_all[...]) * silu_slope(node_pre)).astype(bf16)
+    ndelta_all[own_rows, :] = node_delta
+    ndelta_in = push(
+        "mp", 12, mp_to, lambda peer: ndelta_all.at[own_rows, :], ndelta_all.at[own_rows, :]
+    )
+    agg_back = dot_last(node_delta, nw_in_all[pl.ds(width, width), :])
+    arrived(cot_in)
+    update_grad = cot_rows[...].astype(f32) + repeat_rows(agg_back, degree)
+    gain_part[1:2, :] = jnp.sum(update_grad * edge_hat, axis=0, keepdims=True) * edge_scale
+    edge_slope = local_norm_back(update_grad, e_gain_all[...], edge_hat, edge_rstd).astype(bf16)
+    edge_pre = pre_rows[...].astype(f32)
+    edge_delta = (dot_last(edge_slope, w_out_all[...]) * silu_slope(edge_pre)).astype(bf16)
+    own_edges = rows(me_m, my_edges)
+    delta_all[own_edges, :] = edge_delta
+    delta_in = push(
+        "mp", 13, mp_to, lambda peer: delta_all.at[own_edges, :], delta_all.at[own_edges, :]
+    )
+    eo_part[...] = (dot_first(edge_hidden, edge_slope) * edge_scale).astype(bf16)
+    eo_in = push("mp", 14, mp_to, lambda peer: eo_part.at[:, rows(peer, share)], eo_recv.at[me_m])
+    gain_part_in = push(
+        "mp", 15, mp_to, lambda peer: gain_part.at[:, rows(peer, share)], gain_recv.at[me_m]
+    )
+    eo_recv[me_m] = eo_part[:, own_cols]
+    gain_recv[me_m] = gain_part[:, own_cols]
+
+    arrived(agg_in)
+    arrived(nhid_in)
+    arrived(nslope_in)
+    arrived(ndelta_in)
+    no_send[...] = (dot_first(nhid_all[...], nslope_cols[...]) * node_scale).astype(bf16)
+    ndelta_cols = ndelta_all[:, own_cols]
+    ni_send[pl.ds(0, width), :] = (dot_first(nodes[...], ndelta_cols) * node_scale).astype(bf16)
+    ni_send[pl.ds(width, width), :] = (dot_first(agg_all[...], ndelta_cols) * node_scale).astype(
+        bf16
+    )
+
+    def scatter_sum(kind, parts, landed):
+        size = landed.shape[1]
+        copies = push(
+            "dom", kind, dom_to, lambda peer: parts.at[rows(peer, size), :], landed.at[me_d]
+        )
+        landed[me_d] = parts[rows(me_d, size), :]
+        return copies
+
+    no_in = scatter_sum(1, no_send, no_dom)
+    ni_in = scatter_sum(2, ni_send, ni_dom)
+    total = node_cot[...].astype(f32) + dot_last(ndelta_all[...], nw_in_all[own_cols, :])
+
+    arrived(w_in_in)
+
+    def input_back(owner):
+        block = rows(owner, my_edges)
+        deltas = delta_all[block, :]
+        grad = cot_sorted[block, :].astype(f32) + dot_last(deltas, w_in_rows[0])
+        grad_sorted[block, :] = grad.astype(bf16)
+        back_terms[block, :] = two_terms(dot_last(deltas, w_in_rows[1]))
+        receiver_back[rows(owner, my_nodes), :] = sum_rows(
+            dot_last(deltas, w_in_rows[2]), degree
+        )
+
+    input_back(me_m)
+    for copy, owner in zip(delta_in, mp_from):
+        copy.wait_recv()
+        input_back(owner)
+    sender_sums = join_terms(dot_first(sender_hot[...], back_terms[...]))
+    cross_send[...] = sender_sums[node_count:].astype(bf16)
+    cross_recv[rows(me_d, cap), :] = jnp.zeros((cap, share), bf16)
+    cross_in = push(
+        "dom",
+        3,
+        dom_to,
+        lambda peer: cross_send.at[rows(peer, cap), :],
+        cross_recv.at[rows(me_d, cap), :],
+    )
+    delta_cols = delta_all[:, own_cols]
+    own_scale = jnp.float32(edge_scale)
+    ei_send[pl.ds(0, width), :] = (dot_first(edges_sorted[...], delta_cols) * own_scale).astype(
+        bf16
+    )
+    by_sender = two_terms(dot_first(sender_hot[...], delta_cols))
+    ei_send[pl.ds(width, width), :] = (
+        join_terms(dot_first(extended[...], by_sender)) * own_scale
+    ).astype(bf16)
+    by_receiver = two_terms(sum_rows(delta_cols.astype(f32), degree))
+    ei_send[pl.ds(2 * width, width), :] = (
+        join_terms(dot_first(nodes[...], by_receiver)) * own_scale
+    ).astype(bf16)
+    ei_in = scatter_sum(4, ei_send, ei_dom)
+    arrived(eo_in)
+    eo_send[...] = jnp.sum(eo_recv[...].astype(f32), axis=0).astype(bf16)
+    eo_out = scatter_sum(5, eo_send, eo_dom)
+    arrived(gain_part_in)
+    gain_sum[...] = jnp.sum(gain_recv[...], axis=0)
+    gain_out = push("dom", 6, dom_to, lambda peer: gain_sum, gain_dom.at[me_d])
+    gain_dom[me_d] = gain_sum[...]
+
+    edge_grad[...] = dot_first(perm[...], grad_sorted[...]).astype(bf16)
+    arrived(no_in)
+    node_out_grad[...] = jnp.sum(no_dom[...].astype(f32), axis=0)
+    arrived(ni_in)
+    node_in_grad[...] = jnp.sum(ni_dom[...].astype(f32), axis=0)
+    arrived(cross_in)
+    node_grad[...] = (
+        total + receiver_back[...] + sender_sums[:node_count] + dot_plain(table_hot, cross_recv[...])
+    ).astype(bf16)
+    arrived(gain_out)
+    gains = jnp.sum(gain_dom[...], axis=0)
+    node_gain_grad[...] = gains[0:1]
+    edge_gain_grad[...] = gains[1:2]
+    arrived(eo_out)
+    edge_out_grad[...] = jnp.sum(eo_dom[...].astype(f32), axis=0)
+    arrived(ei_in)
+    edge_in_grad[...] = jnp.sum(ei_dom[...].astype(f32), axis=0)
+    for copy in started:
+        copy.wait_send()
+
+
+def fits_kernel(mesh):
+    return mesh.shape["dom"] * mesh.shape["mp"] <= 16
+
+
+def fused_body(
+    node_latents,
+    edge_latents,
+    node_cotangent,
+    edge_cotangent,
+    senders,
+    receivers,
+    send_nodes,
+    edge_in_weight,
+    edge_out_weight,
+    edge_gain,
+    node_in_weight,
+    node_out_weight,
+    node_gain,
+):
+    dom, mp = lax.axis_size("dom"), lax.axis_size("mp")
+    node_count, width = node_latents.shape
+    edge_count = edge_latents.shape[0]
+    slots = send_nodes.shape[1] * send_nodes.shape[2]
+    share = width // mp
+    my_nodes, my_edges = node_count // mp, edge_count // mp
+    f32, bf16 = jnp.float32, jnp.bfloat16
+    shape = jax.ShapeDtypeStruct
+    outs = (
+        shape((node_count, share), bf16),
+        shape((edge_count, share), bf16),
+        shape((3 * width // dom, share), f32),
+        shape((width // dom, share), f32),
+        shape((1, share), f32),
+        shape((2 * width // dom, share), f32),
+        shape((width // dom, share), f32),
+        shape((1, share), f32),
+    )
+    scratch = [
+        ((slots, width), bf16),
+        ((node_count + slots, width), bf16),
+        ((width, width), bf16),
+        ((2 * width, width), bf16),
+        ((width, width), bf16),
+        ((3, share, width), bf16),
+        ((1, width), f32),
+        ((1, width), f32),
+        ((edge_count, edge_count), bf16),
+        ((edge_count, width), bf16),
+        ((edge_count, share), bf16),
+        ((edge_count, share), bf16),
+        ((edge_count, node_count + slots), bf16),
+        ((edge_count, share), bf16),
+        ((my_edges, width), bf16),
+        ((my_edges, width), bf16),
+        ((my_nodes, width), bf16),
+        ((node_count, width), bf16),
+        ((node_count, width), bf16),
+        ((node_count, width), bf16),
+        ((my_nodes, width), bf16),
+        ((node_count, share), bf16),
+        ((edge_count, width), bf16),
+        ((8, width), f32),
+        ((mp, 8, share), f32),
+        ((8, share), f32),
+        ((dom, 8, share), f32),
+        ((width, width), bf16),
+        ((mp, width, share), bf16),
+        ((width, share), bf16),
+        ((dom, width // dom, share), bf16),
+        ((3 * width, share), bf16),
+        ((dom, 3 * width // dom, share), bf16),
+        ((width, share), bf16),
+        ((dom, width // dom, share), bf16),
+        ((2 * width, share), bf16),
+        ((dom, 2 * width // dom, share), bf16),
+        ((slots, share), bf16),
+        ((slots, share), bf16),
+        ((edge_count, 2 * share), bf16),
+        ((node_count, share), f32),
+    ]
+    vmem = pl.BlockSpec(memory_space=pltpu.VMEM)
+    results = pl.pallas_call(
+        functools.partial(fused_kernel, dom, mp, edge_count // node_count),
+        out_shape=outs,
+        in_specs=[vmem] * 13,
+        out_specs=tuple([vmem] * 8),
+        scratch_shapes=[pltpu.VMEM(dims, kind) for dims, kind in scratch]
+        + [
+            pltpu.SemaphoreType.DMA((16, mp - 1)),
+            pltpu.SemaphoreType.DMA((16, mp - 1)),
+            pltpu.SemaphoreType.DMA((7, dom - 1)),
+            pltpu.SemaphoreType.DMA((7, dom - 1)),
+        ],
+        compiler_params=pltpu.CompilerParams(
+            collective_id=0, has_side_effects=True, vmem_limit_bytes=56 * 1024 * 1024
+        ),
+        name="layer_backward",
+    )(
+        node_latents,
+        edge_latents,
+        node_cotangent,
+        edge_cotangent,
+        senders.reshape(1, edge_count),
+        receivers.reshape(1, edge_count),
+        send_nodes.reshape(1, slots),
+        edge_in_weight.reshape(3, width, share),
+        edge_out_weight,
+        edge_gain.reshape(1, share),
+        node_in_weight,
+        node_out_weight,
+        node_gain.reshape(1, share),
+    )
+    results = list(results)
+    results[4], results[7] = results[4].reshape(share), results[7].reshape(share)
+    return tuple(results)
+
+
 def solution(mesh):
     in_specs = (
         P(("groups", "dom"), None),
@@ -217,4 +738,4 @@
         P(("groups", "dom"), "mp"),
         P(("groups", "mp")),
     )
-    return jax.shard_map(body, mesh=mesh, in_specs=in_specs, out_specs=out_specs, check_vma=False)
+    return jax.shard_map(fused_body if fits_kernel(mesh) else body, mesh=mesh, in_specs=in_specs, out_specs=out_specs, check_vma=False)

time: 270 us -> 80.5 us (0.30)
  waiting for transfers between devices: 120 us -> 0 us
  blocking collectives: 74.3 us -> 0 us
  Pallas kernels: 0 us -> 69.9 us
  matrix products: 20.8 us -> 0 us
  between operations: 14.2 us -> 0.66 us
  local copies, waits for them, and re-layouts: 20.3 us -> 8.4 us
  starting transfers between devices: 11.3 us -> 0 us
  other arithmetic: 8.02 us -> 0 us
    pallas_call x0 -> x1, Pallas kernels: none -> 69.9 us  [fused_body(): pl.pallas_call(functools.partial(fused_kernel, dom, mp, edge_count // nod...]
    reduce_scatter x4 -> x0, waiting for transfers between devices: 59.6 us -> none  [the longest x2 38.3 us: reduce_grads(): lax.psum_scatter(values[0].astype(jnp.bfloat16), 'dom', scatter_dimension...]
    all_gather x5 -> x0, waiting for transfers between devices: 52.8 us -> none  [join_columns(): lax.all_gather(shortened(values), 'mp', axis=1, tiled=True)]
    psum x5 -> x0, blocking collectives: 37.5 us -> none  [the longest x4 25.2 us: row_moments(): lax.psum((jnp.sum(first_term, axis=1), jnp.sum(second_term, axis=1)), 'mp')]
    all_gather x6 -> x0, blocking collectives: 36.8 us -> none  [join_columns(): lax.all_gather(shortened(values), 'mp', axis=1, tiled=True)]
    dot_general x16 -> x0, matrix products: 20.8 us -> none  [the longest x6 8.36 us: dot_first(): lax.dot_general(left, right, (((0,), (0,)), ((), ())), preferred_element_...]
    gather x5 -> x0, local copies, waits for them, and re-layouts: 13.4 us -> none  [the longest x1 3.97 us: body(): node_latents[receivers]]
    all_to_all x2 -> x0, starting transfers between devices: 10.9 us -> none  [swap_crossing(): lax.all_to_all(values, 'dom', split_axis=0, concat_axis=0, tiled=True)]
  transfers between devices with their start and end apart: 11 -> 0, of which waited for: 10 -> 0; matrix products, arithmetic and copies ran while one was open for 9% -> 0% of each run, Pallas kernels for 0% -> 0%
where the time goes in v1:
time: 80.5 us; the launch traced here: 78.9 us
  Pallas kernels  69.9 us (87%)
  local copies, waits for them, and re-layouts  8.4 us (10%)
    pallas_call x1, Pallas kernels, fused_body(): pl.pallas_call(functools.partial(fused_kernel, dom, mp, edge_count // nod...  69.9 us
    unnamed x22, local copies, waits for them, and re-layouts  7.81 us

profile of v1, /device:TPU:0, one launch (start us, length us, event | category | flops | bytes accessed | tf_op | source)
XLA Modules:
  0.0 78.9 jit_solution(15449632574762882202)
XLA Ops:
  0.6 0.0 copy-start.4
  0.6 0.7 copy-done.4
  1.3 0.6 reshape.42.table
  1.9 69.9 %layer_backward.1 = (bf16[128,128]{1,0:T(8,128)(2,1)}, bf16[1024,128]{1,0:T(8,128)(2,1)}, f32[384,128]{1,0:T(8,128)}, f32[128,128]{1,0:T(8,128)}, f32[1,128]{1,0...) custom-call(bf16[128,512]{1,0:T(8,128)(2,1)} %nodes.1, bf16[1024,512]{1,0:T(8,128)(2,1)} %edges.1, ...), custom_call_target="tpu_custom_call" | custom-call | tf_op jit(solution)/shard_map/layer_backward/pallas_call | solution.py:679
  71.8 1.4 %copy.29 = bf16[128,128]{1,0:T(8,128)(2,1)} copy(bf16[128,128]{1,0:T(8,128)(2,1)} %get-tuple-element.32) | data formatting | bytes 65536
  73.2 0.0 copy-start
  73.2 1.7 %copy.30 = bf16[1024,128]{1,0:T(8,128)(2,1)} copy(bf16[1024,128]{1,0:T(8,128)(2,1)} %get-tuple-element.33) | data formatting | bytes 524288
  74.9 0.0 copy-done
  74.9 0.0 copy-start.3
  74.9 0.0 copy-start.6
  74.9 0.7 copy.31
  75.6 0.2 copy-done.3
  75.8 0.0 copy-start.1
  75.8 0.6 copy.32
  76.4 0.0 copy-done.6
  76.4 0.5 copy.33
  76.9 0.0 copy-done.1
  76.9 0.0 copy-start.2
  76.9 0.7 copy.34
  77.6 0.2 copy-done.2
  77.8 0.0 copy-start.5
  77.8 0.6 copy.35
  78.4 0.0 copy-done.5
  78.4 0.5 copy.36
Async XLA Ops:
  0.6 0.7 copy-start.4
  73.2 1.7 %copy-start = (f32[384,128]{1,0:T(8,128)S(1)}, f32[384,128]{1,0:T(8,128)}, u32[]{:S(2)}) copy-start(f32[384,128]{1,0:T(8,128)} %get-tuple-element.34) | copy-start | bytes 589828
  74.9 0.9 %copy-start.3 = (f32[128,128]{1,0:T(8,128)S(1)}, f32[128,128]{1,0:T(8,128)}, u32[]{:S(2)}) copy-start(f32[128,128]{1,0:T(8,128)} %get-tuple-element.35) | copy-start | bytes 196612
  74.9 1.5 %copy-start.6 = (f32[1,128]{1,0:T(1,128)S(1)}, f32[1,128]{1,0:T(1,128)}, u32[]{:S(2)}) copy-start(f32[1,128]{1,0:T(1,128)} %get-tuple-element.20) | copy-start | bytes 1540
  75.8 1.1 %copy-start.1 = (f32[256,128]{1,0:T(8,128)S(1)}, f32[256,128]{1,0:T(8,128)}, u32[]{:S(2)}) copy-start(f32[256,128]{1,0:T(8,128)} %get-tuple-element.37) | copy-start | bytes 393220
  76.9 0.9 %copy-start.2 = (f32[128,128]{1,0:T(8,128)S(1)}, f32[128,128]{1,0:T(8,128)}, u32[]{:S(2)}) copy-start(f32[128,128]{1,0:T(8,128)} %get-tuple-element.38) | copy-start | bytes 196612
  77.8 0.7 copy-start.5

commit v2 on v1

--- a/solution.py
+++ b/solution.py
@@ -306,14 +306,16 @@
     mp_recv_sem,
     dom_send_sem,
     dom_recv_sem,
+    one_send_sem,
+    one_recv_sem,
 ):
     f32, bf16 = jnp.float32, jnp.bfloat16
     node_count, width = nodes.shape
     edge_count = edges.shape[0]
     share = width // mp
     my_nodes, my_edges = node_count // mp, edge_count // mp
-    slots = table.shape[1]
-    cap = slots // dom
+    cap = table.shape[1]
+    slots = dom * cap
     edge_scale = float(edge_count * dom) ** (-0.5)
     node_scale = float(node_count * dom) ** (-0.5)
     me_m, me_d = lax.axis_index("mp"), lax.axis_index("dom")
@@ -321,6 +323,10 @@
     def rows(index, size):
         return pl.ds(pl.multiple_of(index * size, size), size)
 
+    me_g = lax.axis_index("groups")
+    mate = me_m + 1 - 2 * lax.rem(me_m, 2)
+    across = lax.rem(me_m + 2, mp)
+    across_mate = lax.rem(mate + 2, mp)
     mp_to = [lax.rem(me_m + k, mp) for k in range(1, mp)]
     mp_from = [lax.rem(me_m + mp - k, mp) for k in range(1, mp)]
     dom_to = [lax.rem(me_d + k, dom) for k in range(1, dom)]
@@ -346,26 +352,43 @@
         started.extend(copies)
         return copies
 
+    used = iter(range(one_send_sem.shape[0]))
+
+    def put(device, source, target):
+        slot = next(used)
+        copy = pltpu.make_async_remote_copy(
+            src_ref=source,
+            dst_ref=target,
+            send_sem=one_send_sem.at[slot],
+            recv_sem=one_recv_sem.at[slot],
+            device_id=device,
+            device_id_type=pl.DeviceIdType.MESH,
+        )
+        copy.start()
+        started.append(copy)
+        return copy
+
     def arrived(copies):
         for copy in copies:
             copy.wait_recv()
 
     barrier = pltpu.get_barrier_semaphore()
-    for axis, peers in (("mp", mp_to), ("dom", dom_to)):
+    for axis, peers in (("mp", mp_to), ("dom", dom_to), ("groups", [1 - me_g])):
         for peer in peers:
             pl.semaphore_signal(
                 barrier, inc=1, device_id={axis: peer}, device_id_type=pl.DeviceIdType.MESH
             )
 
+    table_row = jnp.concatenate([table[p : p + 1, :] for p in range(dom)], axis=1)
     table_hot = (
-        lax.broadcasted_iota(jnp.int32, (node_count, slots), 0) == table[...]
+        lax.broadcasted_iota(jnp.int32, (node_count, slots), 0) == table_row
     ).astype(bf16)
     halo_send[...] = dot_first(table_hot, nodes[...]).astype(bf16)
     extended[pl.ds(0, node_count), :] = nodes[...]
     extended[pl.ds(pl.multiple_of(node_count + me_d * cap, cap), cap), :] = jnp.zeros(
         (cap, width), bf16
     )
-    pl.semaphore_wait(barrier, mp + dom - 2)
+    pl.semaphore_wait(barrier, mp + dom - 1)
 
     halo = push(
         "dom",
@@ -375,7 +398,31 @@
         extended.at[pl.ds(pl.multiple_of(node_count + me_d * cap, cap), cap), :],
     )
     own_cols = rows(me_m, share)
-    w_out_in = push("mp", 0, mp_to, lambda peer: w_out, w_out_all.at[:, own_cols])
+    across_cols = rows(across, share)
+
+    def weight_first(weight, whole):
+        half = rows(me_g, weight.shape[0] // 2)
+        return [
+            put({"mp": across}, weight.at[half, :], whole.at[half, own_cols]),
+            put({"mp": mate}, weight, whole.at[:, own_cols]),
+        ]
+
+    def weight_second(first, whole):
+        first[0].wait_recv()
+        part = whole.at[rows(me_g, whole.shape[0] // 2), across_cols]
+        return first[1:] + [
+            put({"groups": 1 - me_g}, part, part),
+            put({"mp": mate}, part, part),
+        ]
+
+    def weight_third(second, whole):
+        second[1].wait_recv()
+        part = whole.at[rows(1 - me_g, whole.shape[0] // 2), across_cols]
+        return [second[0], second[2], put({"mp": mate}, part, part)]
+
+    w_out_in = weight_first(w_out, w_out_all)
+    nw_in_in = weight_first(nw_in, nw_in_all)
+    nw_out_in = weight_first(nw_out, nw_out_all)
     gain_in = push("mp", 1, mp_to, lambda peer: e_gain, e_gain_all.at[:, own_cols])
     ngain_in = push("mp", 2, mp_to, lambda peer: n_gain, n_gain_all.at[:, own_cols])
     ncot_in = push(
@@ -418,6 +465,10 @@
         edges_sorted[block, :] = dot_plain(hot, edges[...]).astype(bf16)
         cot_sorted[block, :] = dot_plain(hot, edge_cot[...]).astype(bf16)
         sender_hot[block, :] = dot_last(hot, sender_cols).astype(bf16)
+        if part == mp // 2:
+            w_out_in = weight_second(w_out_in, w_out_all)
+    nw_in_in = weight_second(nw_in_in, nw_in_all)
+    nw_out_in = weight_second(nw_out_in, nw_out_all)
     arrived(halo)
     sender_pre = two_terms(dot_plain(extended[...], w_in[1]))
     for part in range(mp):
@@ -431,8 +482,6 @@
     pre_in = push(
         "mp", 4, mp_to, lambda peer: pre_cols.at[rows(peer, my_edges), :], pre_rows.at[:, own_cols]
     )
-    nw_in_in = push("mp", 6, mp_to, lambda peer: nw_in, nw_in_all.at[:, own_cols])
-    nw_out_in = push("mp", 7, mp_to, lambda peer: nw_out, nw_out_all.at[:, own_cols])
     cot_in = push(
         "mp", 5, mp_to, lambda peer: cot_sorted.at[rows(peer, my_edges), :], cot_rows.at[:, own_cols]
     )
@@ -442,6 +491,7 @@
     pre_rows[:, own_cols] = pre_cols[rows(me_m, my_edges), :]
     cot_rows[:, own_cols] = cot_sorted[rows(me_m, my_edges), :]
 
+    w_out_in = weight_third(w_out_in, w_out_all)
     arrived(pre_in)
     edge_pre = pre_rows[...].astype(f32)
     edge_hidden = (edge_pre * jax.nn.sigmoid(edge_pre)).astype(bf16)
@@ -456,6 +506,8 @@
     agg_in = push(
         "mp", 9, mp_to, lambda peer: agg_all.at[own_rows, :], agg_all.at[own_rows, :]
     )
+    nw_in_in = weight_third(nw_in_in, nw_in_all)
+    nw_out_in = weight_third(nw_out_in, nw_out_all)
     arrived(nw_in_in)
     node_pre = dot_plain(nodes[own_rows, :], nw_in_all[pl.ds(0, width), :]) + dot_plain(
         aggregate, nw_in_all[pl.ds(width, width), :]
@@ -492,16 +544,22 @@
     edge_delta = (dot_last(edge_slope, w_out_all[...]) * silu_slope(edge_pre)).astype(bf16)
     own_edges = rows(me_m, my_edges)
     delta_all[own_edges, :] = edge_delta
-    delta_in = push(
-        "mp", 13, mp_to, lambda peer: delta_all.at[own_edges, :], delta_all.at[own_edges, :]
-    )
+    own_delta = delta_all.at[own_edges, :]
+    delta_across = put({"mp": across}, own_delta, own_delta)
+    delta_mate = put({"mp": mate}, own_delta, own_delta)
     eo_part[...] = (dot_first(edge_hidden, edge_slope) * edge_scale).astype(bf16)
-    eo_in = push("mp", 14, mp_to, lambda peer: eo_part.at[:, rows(peer, share)], eo_recv.at[me_m])
+    eo_in = [
+        put({"mp": mate}, eo_part.at[:, rows(mate, share)], eo_recv.at[0]),
+        put({"mp": mate}, eo_part.at[:, rows(across_mate, share)], eo_recv.at[1]),
+    ]
     gain_part_in = push(
         "mp", 15, mp_to, lambda peer: gain_part.at[:, rows(peer, share)], gain_recv.at[me_m]
     )
-    eo_recv[me_m] = eo_part[:, own_cols]
     gain_recv[me_m] = gain_part[:, own_cols]
+
+    arrived(eo_in)
+    eo_recv[2] = (eo_part[:, across_cols].astype(f32) + eo_recv[1].astype(f32)).astype(bf16)
+    eo_across = put({"mp": across}, eo_recv.at[2], eo_recv.at[3])
 
     arrived(agg_in)
     arrived(nhid_in)
@@ -539,9 +597,14 @@
         )
 
     input_back(me_m)
-    for copy, owner in zip(delta_in, mp_from):
-        copy.wait_recv()
-        input_back(owner)
+    delta_mate.wait_recv()
+    delta_across.wait_recv()
+    across_delta = delta_all.at[rows(across, my_edges), :]
+    delta_last = put({"mp": mate}, across_delta, across_delta)
+    input_back(mate)
+    input_back(across)
+    delta_last.wait_recv()
+    input_back(across_mate)
     sender_sums = join_terms(dot_first(sender_hot[...], back_terms[...]))
     cross_send[...] = sender_sums[node_count:].astype(bf16)
     cross_recv[rows(me_d, cap), :] = jnp.zeros((cap, share), bf16)
@@ -566,8 +629,10 @@
         join_terms(dot_first(nodes[...], by_receiver)) * own_scale
     ).astype(bf16)
     ei_in = scatter_sum(4, ei_send, ei_dom)
-    arrived(eo_in)
-    eo_send[...] = jnp.sum(eo_recv[...].astype(f32), axis=0).astype(bf16)
+    eo_across.wait_recv()
+    eo_send[...] = (
+        eo_part[:, own_cols].astype(f32) + eo_recv[0].astype(f32) + eo_recv[3].astype(f32)
+    ).astype(bf16)
     eo_out = scatter_sum(5, eo_send, eo_dom)
     arrived(gain_part_in)
     gain_sum[...] = jnp.sum(gain_recv[...], axis=0)
@@ -596,7 +661,19 @@
 
 
 def fits_kernel(mesh):
-    return mesh.shape["dom"] * mesh.shape["mp"] <= 16
+    return mesh.shape["groups"] == 2 and mesh.shape["mp"] == 4 and mesh.shape["dom"] <= 8
+
+
+def hand_over_kernel(*refs):
+    count = len(refs) // 2
+    sems = refs[-1]
+    copies = [
+        pltpu.make_async_copy(refs[k], refs[count + k], sems.at[k]) for k in range(count)
+    ]
+    for copy in copies:
+        copy.start()
+    for copy in copies:
+        copy.wait()
 
 
 def fused_body(
@@ -687,6 +764,8 @@
             pltpu.SemaphoreType.DMA((16, mp - 1)),
             pltpu.SemaphoreType.DMA((7, dom - 1)),
             pltpu.SemaphoreType.DMA((7, dom - 1)),
+            pltpu.SemaphoreType.DMA((21,)),
+            pltpu.SemaphoreType.DMA((21,)),
         ],
         compiler_params=pltpu.CompilerParams(
             collective_id=0, has_side_effects=True, vmem_limit_bytes=56 * 1024 * 1024
@@ -699,7 +778,7 @@
         edge_cotangent,
         senders.reshape(1, edge_count),
         receivers.reshape(1, edge_count),
-        send_nodes.reshape(1, slots),
+        send_nodes.reshape(send_nodes.shape[1:]),
         edge_in_weight.reshape(3, width, share),
         edge_out_weight,
         edge_gain.reshape(1, share),
@@ -707,7 +786,17 @@
         node_out_weight,
         node_gain.reshape(1, share),
     )
-    results = list(results)
+    anywhere = pl.BlockSpec(memory_space=pl.ANY)
+    results = list(
+        pl.pallas_call(
+            hand_over_kernel,
+            out_shape=outs,
+            in_specs=[anywhere] * len(outs),
+            out_specs=tuple([anywhere] * len(outs)),
+            scratch_shapes=[pltpu.SemaphoreType.DMA((len(outs),))],
+            name="hand_over",
+        )(*results)
+    )
     results[4], results[7] = results[4].reshape(share), results[7].reshape(share)
     return tuple(results)
 

time: 80.5 us -> 82 us (1.019); the launches traced: 78.9 us -> 81.8 us
  Pallas kernels: 69.9 us -> 81.2 us
  local copies, waits for them, and re-layouts: 8.4 us -> 0 us
    pallas_call x0 -> x1, Pallas kernels: none -> 24 us  [fused_body(): pl.pallas_call(hand_over_kernel, out_shape=outs, in_specs=[anywhere] * le...]
    pallas_call x1, Pallas kernels: 69.9 us -> 57.1 us  [fused_body(): pl.pallas_call(functools.partial(fused_kernel, dom, mp, edge_count // nod...]
    unnamed x22 -> x0, local copies, waits for them, and re-layouts: 7.81 us -> none
where the time goes in v2:
time: 82 us; the launch traced here: 81.8 us
  Pallas kernels  81.2 us (99%)
    pallas_call x1, Pallas kernels, fused_body(): pl.pallas_call(functools.partial(fused_kernel, dom, mp, edge_count // nod...  57.1 us
    pallas_call x1, Pallas kernels, fused_body(): pl.pallas_call(hand_over_kernel, out_shape=outs, in_specs=[anywhere] * le...  24 us

profile of v2, /device:TPU:0, one launch (start us, length us, event | category | flops | bytes accessed | tf_op | source)
XLA Modules:
  0.0 81.8 jit_solution(15532597517058520457)
XLA Ops:
  0.6 57.1 %layer_backward.1 = (bf16[128,128]{1,0:T(8,128)(2,1)}, bf16[1024,128]{1,0:T(8,128)(2,1)}, f32[384,128]{1,0:T(8,128)}, f32[128,128]{1,0:T(8,128)}, f32[1,128]{1,0...) custom-call(bf16[128,512]{1,0:T(8,128)(2,1)} %nodes.1, bf16[1024,512]{1,0:T(8,128)(2,1)} %edges.1, ...), custom_call_target="tpu_custom_call" | custom-call | tf_op jit(solution)/shard_map/layer_backward/pallas_call | solution.py:756
  57.8 24.0 %hand_over.1 = (bf16[128,128]{1,0:T(8,128)(2,1)}, bf16[1024,128]{1,0:T(8,128)(2,1)}, f32[384,128]{1,0:T(8,128)}, f32[128,128]{1,0:T(8,128)}, f32[1,128]{1,0:T(1,...) custom-call(bf16[128,128]{1,0:T(8,128)(2,1)} %get-tuple-element.24.refs_0_, ...), custom_call_target="tpu_custom_call" | custom-call | tf_op jit(solution)/shard_map/hand_over/pallas_call | solution.py:791

commit v3 on v2

--- a/solution.py
+++ b/solution.py
@@ -302,6 +302,7 @@
     cross_recv,
     back_terms,
     receiver_back,
+    receiver_pre,
     mp_send_sem,
     mp_recv_sem,
     dom_send_sem,
@@ -455,44 +456,43 @@
     sender_cols = (
         lax.broadcasted_iota(jnp.int32, (node_count + slots, edge_count), 0) == senders[...]
     ).astype(bf16)
-    receiver_pre = dot_plain(nodes[...], w_in[2])
-    for part in range(mp):
-        block = pl.ds(part * my_edges, my_edges)
+    receiver_pre[...] = dot_plain(nodes[...], w_in[2])
+    owners = [across, across_mate, mate, me_m]
+    cot_in = []
+    for step, owner in enumerate(owners):
+        block = rows(owner, my_edges)
         hot = (
-            lax.broadcasted_iota(jnp.int32, (my_edges, edge_count), 0) + part * my_edges == place
+            lax.broadcasted_iota(jnp.int32, (my_edges, edge_count), 0) + owner * my_edges == place
         ).astype(bf16)
         perm[block, :] = hot
+        cot_sorted[block, :] = dot_plain(hot, edge_cot[...]).astype(bf16)
+        if step < mp - 1:
+            cot_in.append(put({"mp": owner}, cot_sorted.at[block, :], cot_rows.at[:, own_cols]))
         edges_sorted[block, :] = dot_plain(hot, edges[...]).astype(bf16)
-        cot_sorted[block, :] = dot_plain(hot, edge_cot[...]).astype(bf16)
         sender_hot[block, :] = dot_last(hot, sender_cols).astype(bf16)
-        if part == mp // 2:
+        if step == mp // 2:
             w_out_in = weight_second(w_out_in, w_out_all)
     nw_in_in = weight_second(nw_in_in, nw_in_all)
     nw_out_in = weight_second(nw_out_in, nw_out_all)
     arrived(halo)
     sender_pre = two_terms(dot_plain(extended[...], w_in[1]))
-    for part in range(mp):
-        block = pl.ds(part * my_edges, my_edges)
+    pre_in = []
+    for step, owner in enumerate(owners):
+        block = rows(owner, my_edges)
         local = dot_plain(edges_sorted[block, :], w_in[0])
-        local = local + repeat_rows(
-            receiver_pre[part * my_nodes : (part + 1) * my_nodes], degree
-        )
+        local = local + repeat_rows(receiver_pre[rows(owner, my_nodes), :], degree)
         local = local + join_terms(dot_plain(sender_hot[block, :], sender_pre))
         pre_cols[block, :] = local.astype(bf16)
-    pre_in = push(
-        "mp", 4, mp_to, lambda peer: pre_cols.at[rows(peer, my_edges), :], pre_rows.at[:, own_cols]
-    )
-    cot_in = push(
-        "mp", 5, mp_to, lambda peer: cot_sorted.at[rows(peer, my_edges), :], cot_rows.at[:, own_cols]
-    )
+        if step < mp - 1:
+            pre_in.append(put({"mp": owner}, pre_cols.at[block, :], pre_rows.at[:, own_cols]))
+    pre_rows[:, own_cols] = pre_cols[rows(me_m, my_edges), :]
+    cot_rows[:, own_cols] = cot_sorted[rows(me_m, my_edges), :]
+
+    w_out_in = weight_third(w_out_in, w_out_all)
+    arrived(pre_in)
     w_in_in = push(
         "mp", 8, mp_to, lambda peer: w_in.at[:, rows(peer, share), :], w_in_rows.at[:, :, own_cols]
     )
-    pre_rows[:, own_cols] = pre_cols[rows(me_m, my_edges), :]
-    cot_rows[:, own_cols] = cot_sorted[rows(me_m, my_edges), :]
-
-    w_out_in = weight_third(w_out_in, w_out_all)
-    arrived(pre_in)
     edge_pre = pre_rows[...].astype(f32)
     edge_hidden = (edge_pre * jax.nn.sigmoid(edge_pre)).astype(bf16)
     arrived(w_out_in)
@@ -544,22 +544,19 @@
     edge_delta = (dot_last(edge_slope, w_out_all[...]) * silu_slope(edge_pre)).astype(bf16)
     own_edges = rows(me_m, my_edges)
     delta_all[own_edges, :] = edge_delta
+    cols = [rows(owner, share) for owner in owners]
+
+    def delta_piece(device, owner, col):
+        piece = delta_all.at[rows(owner, my_edges), col]
+        return put({"mp": device}, piece, piece)
+
+    delta_own_cols = [delta_piece(across, me_m, cols[0]), delta_piece(across_mate, me_m, cols[1])]
     own_delta = delta_all.at[own_edges, :]
-    delta_across = put({"mp": across}, own_delta, own_delta)
     delta_mate = put({"mp": mate}, own_delta, own_delta)
-    eo_part[...] = (dot_first(edge_hidden, edge_slope) * edge_scale).astype(bf16)
-    eo_in = [
-        put({"mp": mate}, eo_part.at[:, rows(mate, share)], eo_recv.at[0]),
-        put({"mp": mate}, eo_part.at[:, rows(across_mate, share)], eo_recv.at[1]),
-    ]
     gain_part_in = push(
         "mp", 15, mp_to, lambda peer: gain_part.at[:, rows(peer, share)], gain_recv.at[me_m]
     )
     gain_recv[me_m] = gain_part[:, own_cols]
-
-    arrived(eo_in)
-    eo_recv[2] = (eo_part[:, across_cols].astype(f32) + eo_recv[1].astype(f32)).astype(bf16)
-    eo_across = put({"mp": across}, eo_recv.at[2], eo_recv.at[3])
 
     arrived(agg_in)
     arrived(nhid_in)
@@ -584,6 +581,32 @@
     ni_in = scatter_sum(2, ni_send, ni_dom)
     total = node_cot[...].astype(f32) + dot_last(ndelta_all[...], nw_in_all[own_cols, :])
 
+    eo_part[...] = (dot_first(edge_hidden, edge_slope) * edge_scale).astype(bf16)
+    eo_in = [
+        put({"mp": mate}, eo_part.at[:, rows(mate, share)], eo_recv.at[0]),
+        put({"mp": mate}, eo_part.at[:, rows(across_mate, share)], eo_recv.at[1]),
+    ]
+    delta_rest = [delta_piece(across, me_m, col) for col in cols[1:]]
+    delta_mate.wait_recv()
+    arrived(delta_own_cols)
+    delta_cols = delta_all[:, own_cols]
+    own_scale = jnp.float32(edge_scale)
+    ei_send[pl.ds(0, width), :] = (dot_first(edges_sorted[...], delta_cols) * own_scale).astype(
+        bf16
+    )
+    by_sender = two_terms(dot_first(sender_hot[...], delta_cols))
+    ei_send[pl.ds(width, width), :] = (
+        join_terms(dot_first(extended[...], by_sender)) * own_scale
+    ).astype(bf16)
+    by_receiver = two_terms(sum_rows(delta_cols.astype(f32), degree))
+    ei_send[pl.ds(2 * width, width), :] = (
+        join_terms(dot_first(nodes[...], by_receiver)) * own_scale
+    ).astype(bf16)
+    ei_in = scatter_sum(4, ei_send, ei_dom)
+    arrived(eo_in)
+    eo_recv[2] = (eo_part[:, across_cols].astype(f32) + eo_recv[1].astype(f32)).astype(bf16)
+    eo_across = put({"mp": across}, eo_recv.at[2], eo_recv.at[3])
+
     arrived(w_in_in)
 
     def input_back(owner):
@@ -597,13 +620,16 @@
         )
 
     input_back(me_m)
-    delta_mate.wait_recv()
-    delta_across.wait_recv()
-    across_delta = delta_all.at[rows(across, my_edges), :]
-    delta_last = put({"mp": mate}, across_delta, across_delta)
     input_back(mate)
+    arrived(delta_rest)
+    delta_last = [delta_piece(mate, across, col) for col in (cols[3], cols[0], cols[1])]
+    eo_across.wait_recv()
+    eo_send[...] = (
+        eo_part[:, own_cols].astype(f32) + eo_recv[0].astype(f32) + eo_recv[3].astype(f32)
+    ).astype(bf16)
+    eo_out = scatter_sum(5, eo_send, eo_dom)
     input_back(across)
-    delta_last.wait_recv()
+    arrived(delta_last)
     input_back(across_mate)
     sender_sums = join_terms(dot_first(sender_hot[...], back_terms[...]))
     cross_send[...] = sender_sums[node_count:].astype(bf16)
@@ -615,25 +641,6 @@
         lambda peer: cross_send.at[rows(peer, cap), :],
         cross_recv.at[rows(me_d, cap), :],
     )
-    delta_cols = delta_all[:, own_cols]
-    own_scale = jnp.float32(edge_scale)
-    ei_send[pl.ds(0, width), :] = (dot_first(edges_sorted[...], delta_cols) * own_scale).astype(
-        bf16
-    )
-    by_sender = two_terms(dot_first(sender_hot[...], delta_cols))
-    ei_send[pl.ds(width, width), :] = (
-        join_terms(dot_first(extended[...], by_sender)) * own_scale
-    ).astype(bf16)
-    by_receiver = two_terms(sum_rows(delta_cols.astype(f32), degree))
-    ei_send[pl.ds(2 * width, width), :] = (
-        join_terms(dot_first(nodes[...], by_receiver)) * own_scale
-    ).astype(bf16)
-    ei_in = scatter_sum(4, ei_send, ei_dom)
-    eo_across.wait_recv()
-    eo_send[...] = (
-        eo_part[:, own_cols].astype(f32) + eo_recv[0].astype(f32) + eo_recv[3].astype(f32)
-    ).astype(bf16)
-    eo_out = scatter_sum(5, eo_send, eo_dom)
     arrived(gain_part_in)
     gain_sum[...] = jnp.sum(gain_recv[...], axis=0)
     gain_out = push("dom", 6, dom_to, lambda peer: gain_sum, gain_dom.at[me_d])
@@ -666,14 +673,8 @@
 
 def hand_over_kernel(*refs):
     count = len(refs) // 2
-    sems = refs[-1]
-    copies = [
-        pltpu.make_async_copy(refs[k], refs[count + k], sems.at[k]) for k in range(count)
-    ]
-    for copy in copies:
-        copy.start()
-    for copy in copies:
-        copy.wait()
+    for source, target in zip(refs[:count], refs[count:]):
+        target[...] = source[...]
 
 
 def fused_body(
@@ -751,6 +752,7 @@
         ((slots, share), bf16),
         ((edge_count, 2 * share), bf16),
         ((node_count, share), f32),
+        ((node_count, share), f32),
     ]
     vmem = pl.BlockSpec(memory_space=pltpu.VMEM)
     results = pl.pallas_call(
@@ -764,8 +766,8 @@
             pltpu.SemaphoreType.DMA((16, mp - 1)),
             pltpu.SemaphoreType.DMA((7, dom - 1)),
             pltpu.SemaphoreType.DMA((7, dom - 1)),
-            pltpu.SemaphoreType.DMA((21,)),
-            pltpu.SemaphoreType.DMA((21,)),
+            pltpu.SemaphoreType.DMA((40,)),
+            pltpu.SemaphoreType.DMA((40,)),
         ],
         compiler_params=pltpu.CompilerParams(
             collective_id=0, has_side_effects=True, vmem_limit_bytes=56 * 1024 * 1024
@@ -786,14 +788,12 @@
         node_out_weight,
         node_gain.reshape(1, share),
     )
-    anywhere = pl.BlockSpec(memory_space=pl.ANY)
     results = list(
         pl.pallas_call(
             hand_over_kernel,
             out_shape=outs,
-            in_specs=[anywhere] * len(outs),
-            out_specs=tuple([anywhere] * len(outs)),
-            scratch_shapes=[pltpu.SemaphoreType.DMA((len(outs),))],
+            in_specs=[vmem] * len(outs),
+            out_specs=tuple([vmem] * len(outs)),
             name="hand_over",
         )(*results)
     )

time: 82 us -> 59.1 us (0.72)
  Pallas kernels: 81.2 us -> 58.3 us
    pallas_call x1, Pallas kernels: 24 us -> 2.01 us  [fused_body(): pl.pallas_call(hand_over_kernel, out_shape=outs, in_specs=[vmem] * len(ou...]
    pallas_call x1, Pallas kernels: 57.1 us -> 56.2 us  [fused_body(): pl.pallas_call(functools.partial(fused_kernel, dom, mp, edge_count // nod...]
where the time goes in v3:
time: 59.1 us; the launch traced here: 58.9 us
  Pallas kernels  58.3 us (99%)
  between operations  0.65 us (1%)
    pallas_call x1, Pallas kernels, fused_body(): pl.pallas_call(functools.partial(fused_kernel, dom, mp, edge_count // nod...  56.2 us
    pallas_call x1, Pallas kernels, fused_body(): pl.pallas_call(hand_over_kernel, out_shape=outs, in_specs=[vmem] * len(ou...  2.01 us

profile of v3, /device:TPU:0, one launch (start us, length us, event | category | flops | bytes accessed | tf_op | source)
XLA Modules:
  0.0 58.9 jit_solution(292915316039340378)
XLA Ops:
  0.6 56.2 %layer_backward.1 = (bf16[128,128]{1,0:T(8,128)(2,1)}, bf16[1024,128]{1,0:T(8,128)(2,1)}, f32[384,128]{1,0:T(8,128)}, f32[128,128]{1,0:T(8,128)}, f32[1,128]{1,0...) custom-call(bf16[128,512]{1,0:T(8,128)(2,1)} %nodes.1, bf16[1024,512]{1,0:T(8,128)(2,1)} %edges.1, ...), custom_call_target="tpu_custom_call" | custom-call | tf_op jit(solution)/shard_map/layer_backward/pallas_call | solution.py:758
  56.9 2.0 %hand_over.1 = (bf16[128,128]{1,0:T(8,128)(2,1)}, bf16[1024,128]{1,0:T(8,128)(2,1)}, f32[384,128]{1,0:T(8,128)}, f32[128,128]{1,0:T(8,128)}, f32[1,128]{1,0:T(1,...) custom-call(bf16[128,128]{1,0:T(8,128)(2,1)} %get-tuple-element.24.refs_0_, ...), custom_call_target="tpu_custom_call" | custom-call | tf_op jit(solution)/shard_map/hand_over/pallas_call | solution.py:792

commit v4 on v3

--- a/solution.py
+++ b/solution.py
@@ -553,6 +553,12 @@
     delta_own_cols = [delta_piece(across, me_m, cols[0]), delta_piece(across_mate, me_m, cols[1])]
     own_delta = delta_all.at[own_edges, :]
     delta_mate = put({"mp": mate}, own_delta, own_delta)
+    eo_part[...] = (dot_first(edge_hidden, edge_slope) * edge_scale).astype(bf16)
+    eo_in = [
+        put({"mp": mate}, eo_part.at[:, rows(mate, share)], eo_recv.at[0]),
+        put({"mp": mate}, eo_part.at[:, rows(across_mate, share)], eo_recv.at[1]),
+    ]
+    delta_rest = [delta_piece(across, me_m, col) for col in cols[1:]]
     gain_part_in = push(
         "mp", 15, mp_to, lambda peer: gain_part.at[:, rows(peer, share)], gain_recv.at[me_m]
     )
@@ -581,12 +587,6 @@
     ni_in = scatter_sum(2, ni_send, ni_dom)
     total = node_cot[...].astype(f32) + dot_last(ndelta_all[...], nw_in_all[own_cols, :])
 
-    eo_part[...] = (dot_first(edge_hidden, edge_slope) * edge_scale).astype(bf16)
-    eo_in = [
-        put({"mp": mate}, eo_part.at[:, rows(mate, share)], eo_recv.at[0]),
-        put({"mp": mate}, eo_part.at[:, rows(across_mate, share)], eo_recv.at[1]),
-    ]
-    delta_rest = [delta_piece(across, me_m, col) for col in cols[1:]]
     delta_mate.wait_recv()
     arrived(delta_own_cols)
     delta_cols = delta_all[:, own_cols]

time: 59.1 us -> 59.1 us (level)
  no operation moved by 1% of the time
where the time goes in v4:
time: 59.1 us; the launch traced here: 58.9 us
  Pallas kernels  58.3 us (99%)
  between operations  0.65 us (1%)
    pallas_call x1, Pallas kernels, fused_body(): pl.pallas_call(functools.partial(fused_kernel, dom, mp, edge_count // nod...  56.2 us
    pallas_call x1, Pallas kernels, fused_body(): pl.pallas_call(hand_over_kernel, out_shape=outs, in_specs=[vmem] * len(ou...  2.01 us

profile of v4, /device:TPU:0, one launch (start us, length us, event | category | flops | bytes accessed | tf_op | source)
XLA Modules:
  0.0 58.9 jit_solution(8270213539386147943)
XLA Ops:
  0.6 56.2 %layer_backward.1 = (bf16[128,128]{1,0:T(8,128)(2,1)}, bf16[1024,128]{1,0:T(8,128)(2,1)}, f32[384,128]{1,0:T(8,128)}, f32[128,128]{1,0:T(8,128)}, f32[1,128]{1,0...) custom-call(bf16[128,512]{1,0:T(8,128)(2,1)} %nodes.1, bf16[1024,512]{1,0:T(8,128)(2,1)} %edges.1, ...), custom_call_target="tpu_custom_call" | custom-call | tf_op jit(solution)/shard_map/layer_backward/pallas_call | solution.py:758
  56.9 2.0 %hand_over.1 = (bf16[128,128]{1,0:T(8,128)(2,1)}, bf16[1024,128]{1,0:T(8,128)(2,1)}, f32[384,128]{1,0:T(8,128)}, f32[128,128]{1,0:T(8,128)}, f32[1,128]{1,0:T(1,...) custom-call(bf16[128,128]{1,0:T(8,128)(2,1)} %get-tuple-element.24.refs_0_, ...), custom_call_target="tpu_custom_call" | custom-call | tf_op jit(solution)/shard_map/hand_over/pallas_call | solution.py:792
